TPU v7x, 32 devices: a whole 2x2x4 slice. The times are simulated.
32 devices in a mesh: groups: 2 (over x), tensor: 8 (over z, y), side: 2 (over core).
Axes of the slice: x: 2, y: 2, z: 4, core: 2. Of those that a mesh axis runs over, the one named last changes fastest.
Arguments:
- hidden: bfloat16 [4, 64, 5120], P(None, ('groups', 'tensor', 'side')), parts along dimension 1, may hold values from -6 to 6
- norm_gain: float32 [5120], replicated, may hold values from 0.5 to 1.5
- query_gain: float32 [128], replicated, may hold values from 0.5 to 120
- key_gain: float32 [128], replicated, may hold values from 0.5 to 3
- w_query: bfloat16 [5120, 8192], P(('tensor', 'side')), may hold values from -0.078125 to 0.078125
- w_key: bfloat16 [5120, 1024], P(('tensor', 'side')), may hold values from -0.078125 to 0.078125
- w_value: bfloat16 [5120, 1024], P(('tensor', 'side')), may hold values from -0.078125 to 0.078125
- w_out: bfloat16 [8192, 5120], P(None, ('tensor', 'side')), may hold values from -0.0625 to 0.0625
- cache_k: bfloat16 [64, 8, 512, 128], P(('groups', 'tensor', 'side')), parts along dimension 0, may hold values from -6 to 6
- cache_v: bfloat16 [64, 8, 512, 128], P(('groups', 'tensor', 'side')), parts along dimension 0, may hold values from -6 to 6
- lengths: int32 [64], P(('groups', 'tensor', 'side')), parts along dimension 0, may hold values from 1 to 512, 8192 in all
Outputs:
- layer_out: bfloat16 [4, 64, 5120], P(None, ('groups', 'tensor', 'side')), parts along dimension 1
There are 2 independent parts, one for each index of `groups`. A program takes and returns all parts, laid end to end along the dimension named above; an argument that names none is the same for every part. Nothing has to cross between parts.
Inputs may be any that keep to these rules, and one draw needn't show every extreme that they name: `lengths`: each row's count of cached positions in use; within each job the 32 rows' counts sum to 8192, and in each job the largest row uses all 512.
All inputs are finite; a program needn't handle non-finite values. No bound on the sum of `lengths` on one device may be relied on, other than what follows from the above.
Results may differ from a plain program's by a relative error of at most 0.013.
The roundings to bfloat16 on the way count: a program that leaves them out, or rounds other values in their place, can miss the bound.
Values may be sent and summed in bfloat16 or wider, within the bound.
A program may use at most 192 MiB of HBM per device.

v0:
```python
import jax
import jax.numpy as jnp
from jax import lax
from jax.sharding import PartitionSpec as P

rope_base = 1000000.0
norm_eps = 1e-06
masked_score = -1e30


def rms_scale(values, gain_vector):
    mean_square = jnp.mean(values * values, axis=-1, keepdims=True)
    return values * lax.rsqrt(mean_square + norm_eps) * gain_vector


def rotate(values, positions):
    half_dim = values.shape[-1] // 2
    frequency = rope_base ** (-2.0 * jnp.arange(half_dim, dtype=jnp.float32) / values.shape[-1])
    angles = positions[:, None] * frequency[None, :]
    cosine = jnp.cos(angles)[:, None, :]
    sine_part = jnp.sin(angles)[:, None, :]
    lower_half = values[..., :half_dim]
    upper_half = values[..., half_dim:]
    return jnp.concatenate(
        [
            lower_half * cosine - upper_half * sine_part,
            upper_half * cosine + lower_half * sine_part,
        ],
        axis=-1,
    )


def attend(queries, cache_k, cache_v, lengths, fresh_k, fresh_v):
    row_count, head_count, head_size = queries.shape
    kv_count = cache_k.shape[1]
    grouped = queries.reshape(row_count, kv_count, head_count // kv_count, head_size)
    score_scale = head_size ** (-0.5)
    cached_scores = (
        jnp.einsum("rkgd,rkld->rkgl", grouped, cache_k, preferred_element_type=jnp.float32)
        * score_scale
    )
    live_mask = jnp.arange(cache_k.shape[2], dtype=jnp.int32)[None, :] < lengths[:, None]
    cached_scores = jnp.where(live_mask[:, None, None, :], cached_scores, masked_score)
    fresh_scores = (
        jnp.einsum("rkgd,rksd->rkgs", grouped, fresh_k, preferred_element_type=jnp.float32)
        * score_scale
    )
    highest = jnp.maximum(jnp.max(cached_scores, axis=-1), jnp.max(fresh_scores, axis=-1))[
        ..., None
    ]
    cached_exp = jnp.exp(cached_scores - highest)
    fresh_exp = jnp.exp(fresh_scores - highest)
    denominator = jnp.sum(cached_exp, axis=-1, keepdims=True) + jnp.sum(
        fresh_exp, axis=-1, keepdims=True
    )
    cached_weight = (cached_exp / denominator).astype(jnp.bfloat16)
    fresh_weight = (fresh_exp / denominator).astype(jnp.bfloat16)
    mixed_out = jnp.einsum(
        "rkgl,rkld->rkgd", cached_weight, cache_v, preferred_element_type=jnp.float32
    )
    mixed_out = mixed_out + jnp.einsum(
        "rkgs,rksd->rkgd", fresh_weight, fresh_v, preferred_element_type=jnp.float32
    )
    return mixed_out.reshape(row_count, head_count * head_size).astype(jnp.bfloat16)


def body(
    hidden,
    norm_gain,
    query_gain,
    key_gain,
    w_query,
    w_key,
    w_value,
    w_out,
    cache_k,
    cache_v,
    lengths,
):
    step_total, row_count, model_width = hidden.shape
    relayed = (
        lax.all_gather(w_query, "side", axis=0, tiled=True),
        lax.all_gather(w_key, "side", axis=0, tiled=True),
        lax.all_gather(w_value, "side", axis=0, tiled=True),
    )
    query_weight, key_weight, value_weight = (
        lax.all_to_all(relayed[0], "tensor", split_axis=1, concat_axis=0, tiled=True),
        lax.all_to_all(relayed[1], "tensor", split_axis=1, concat_axis=0, tiled=True),
        lax.all_to_all(relayed[2], "tensor", split_axis=1, concat_axis=0, tiled=True),
    )
    joined_weight = jnp.concatenate([query_weight, key_weight, value_weight], axis=1)
    query_cols = query_weight.shape[1]
    key_cols = key_weight.shape[1]
    out_weight = lax.all_gather(w_out, "side", axis=1, tiled=True)
    out_weight = lax.all_to_all(out_weight, "tensor", split_axis=0, concat_axis=1, tiled=True)
    head_size = query_gain.shape[0]
    positions = lengths.astype(jnp.float32)
    fresh_keys = []
    fresh_values = []
    outputs = []
    for step_index in range(step_total):
        residual = hidden[step_index].astype(jnp.float32)
        normed = rms_scale(residual, norm_gain).astype(jnp.bfloat16)
        projected = jnp.dot(
            lax.all_gather(normed, "tensor", axis=0, tiled=True),
            joined_weight,
            preferred_element_type=jnp.float32,
        ).astype(jnp.bfloat16)
        q_part = projected[:, :query_cols]
        k_part = projected[:, query_cols : query_cols + key_cols]
        v_part = projected[:, query_cols + key_cols :]
        q_rows, k_rows, v_rows = (
            lax.all_to_all(q_part, "tensor", split_axis=0, concat_axis=1, tiled=True),
            lax.all_to_all(k_part, "tensor", split_axis=0, concat_axis=1, tiled=True),
            lax.all_to_all(v_part, "tensor", split_axis=0, concat_axis=1, tiled=True),
        )
        head_count = q_rows.shape[1] // head_size
        kv_count = k_rows.shape[1] // head_size
        q_heads = q_rows.astype(jnp.float32).reshape(row_count, head_count, head_size)
        k_heads = k_rows.astype(jnp.float32).reshape(row_count, kv_count, head_size)
        queries = rotate(rms_scale(q_heads, query_gain), positions + step_index).astype(
            jnp.bfloat16
        )
        keys_new = rotate(rms_scale(k_heads, key_gain), positions + step_index).astype(jnp.bfloat16)
        fresh_keys.append(keys_new)
        fresh_values.append(v_rows.reshape(row_count, kv_count, head_size))
        attended = attend(
            queries,
            cache_k,
            cache_v,
            lengths,
            jnp.stack(fresh_keys, axis=2),
            jnp.stack(fresh_values, axis=2),
        )
        head_layout = lax.all_to_all(attended, "tensor", split_axis=1, concat_axis=0, tiled=True)
        update = lax.psum_scatter(
            jnp.dot(head_layout, out_weight, preferred_element_type=jnp.float32).astype(
                jnp.bfloat16
            ),
            "tensor",
            scatter_dimension=0,
            tiled=True,
        ).astype(jnp.float32)
        outputs.append((residual + update).astype(jnp.bfloat16))
    return jnp.stack(outputs, axis=0)


def solution(mesh):
    placed = (
        P(None, ("groups", "tensor", "side"), None),
        P(),
        P(),
        P(),
        P(("tensor", "side"), None),
        P(("tensor", "side"), None),
        P(("tensor", "side"), None),
        P(None, ("tensor", "side")),
        P(("groups", "tensor", "side"), None, None, None),
        P(("groups", "tensor", "side"), None, None, None),
        P(("groups", "tensor", "side")),
    )
    return jax.shard_map(
        body,
        mesh=mesh,
        in_specs=placed,
        out_specs=P(None, ("groups", "tensor", "side"), None),
        check_vma=False,
    )
```

profile of v0, /device:TPU:0, one launch (start us, length us, event | category | flops | bytes accessed | tf_op | source)
XLA Modules:
  0.0 1011.1 jit_solution(2259967136571706138)
XLA Ops:
  8.7 12.3 %all-gather.13.cloned.1.call-done = bf16[640,1024]{1,0:T(8,128)(2,1)} async-done(((bf16[320,1024]{1,0:T(8,128)(2,1)}), bf16[640,1024]{1,0:T(8,128)(2,1)}) %all-gather.13.cloned.1.call-update) | async-done | bytes 1310736 | tf_op jit(solution)/shard_map/all_gather | solution.py:84
  35.6 25.5 %all-to-all-done.2 = bf16[640,8,128]{0,2,1:T(8,128)(2,1)S(1)} async-done(((bf16[640,8,128]{0,2,1:T(8,128)(2,1)}), bf16[640,8,128]{0,2,1:T(8,128)(2,1)S(1)}, u32[]{:S(2)}, u32[]{:S(2)}) %all-to-all-start.2) | async-done | bytes 1310752 | tf_op jit(solution)/shard_map/all_to_all | solution.py:89
  65.4 14.3 %copy.341 = bf16[640,8192]{0,1:T(8,128)(2,1)} copy(bf16[640,8192]{1,0:T(8,128)(2,1)} %all-gather.9.cloned.1.call-done) | data formatting | bytes 20971520 | tf_op jit(solution)/shard_map/all_gather | solution.py:82
  79.7 16.7 %all-to-all-done.1 = bf16[640,8,128]{0,2,1:T(8,128)(2,1)} async-done(((bf16[640,8,128]{0,2,1:T(8,128)(2,1)}), bf16[640,8,128]{0,2,1:T(8,128)(2,1)}, u32[]{:S(2)}, u32[]{:S(2)}) %all-to-all-start.1) | async-done | bytes 1310752 | tf_op jit(solution)/shard_map/all_to_all | solution.py:88
  102.2 25.7 %all-gather.15.cloned.1.call-done = bf16[8192,640]{0,1:T(8,128)(2,1)} async-done(((bf16[8192,320]{0,1:T(8,128)(2,1)}), bf16[8192,640]{0,1:T(8,128)(2,1)}) %all-gather.15.cloned.1.call-update) | async-done | bytes 10485776 | tf_op jit(solution)/shard_map/all_gather | solution.py:94
  127.9 14.4 %copy.351 = bf16[8192,640]{1,0:T(8,128)(2,1)} copy(bf16[8192,640]{0,1:T(8,128)(2,1)} %all-gather.15.cloned.1.call-done) | data formatting | bytes 20971520 | tf_op jit(solution)/shard_map/all_gather | solution.py:94
  142.3 186.0 %all-to-all-done = bf16[640,8,1024]{0,2,1:T(8,128)(2,1)} async-done(((bf16[640,8,1024]{0,2,1:T(8,128)(2,1)}), bf16[640,8,1024]{0,2,1:T(8,128)(2,1)}, u32[]{:S(2)}, u32[]{:S(2)}) %all-to-all-start) | async-done | bytes 10485792 | tf_op jit(solution)/shard_map/all_to_all | solution.py:87
  334.7 247.8 %all-gather.3 = bf16[8,2,5120]{2,1,0:T(2,128)(2,1)} all-gather(bf16[1,2,5120]{2,1,0:T(2,128)(2,1)S(1)} %get-tuple-element.16), channel_id=1, replica_groups=mesh['groups'=2,'tensor'=8,'side'=2] {'tensor'}, dimensions={0}, use_global_device_ids=true | all-gather | bytes 184320 | tf_op jit(solution)/shard_map/all_gather | solution.py:105
  584.1 32.6 %all-gather.2 = bf16[8,2,5120]{2,1,0:T(2,128)(2,1)} all-gather(bf16[1,2,5120]{2,1,0:T(2,128)(2,1)S(1)} %get-tuple-element.15), channel_id=1, replica_groups=mesh['groups'=2,'tensor'=8,'side'=2] {'tensor'}, dimensions={0}, use_global_device_ids=true | all-gather | bytes 184320 | tf_op jit(solution)/shard_map/all_gather | solution.py:105
  618.4 32.8 %all-gather.1 = bf16[8,2,5120]{2,1,0:T(2,128)(2,1)} all-gather(bf16[1,2,5120]{2,1,0:T(2,128)(2,1)S(1)} %get-tuple-element.14), channel_id=1, replica_groups=mesh['groups'=2,'tensor'=8,'side'=2] {'tensor'}, dimensions={0}, use_global_device_ids=true | all-gather | bytes 184320 | tf_op jit(solution)/shard_map/all_gather | solution.py:105
  652.8 32.6 %all-gather = bf16[8,2,5120]{2,1,0:T(2,128)(2,1)} all-gather(bf16[1,2,5120]{2,1,0:T(2,128)(2,1)S(1)} %get-tuple-element.13), channel_id=1, replica_groups=mesh['groups'=2,'tensor'=8,'side'=2] {'tensor'}, dimensions={0}, use_global_device_ids=true | all-gather | bytes 184320 | tf_op jit(solution)/shard_map/all_gather | solution.py:105
  691.7 15.2 %copy.342 = bf16[8,640,1024]{2,1,0:T(8,128)(2,1)} copy(bf16[8,640,1024]{1,2,0:T(8,128)(2,1)} %bitcast.4) | data formatting | bytes 20971520 | tf_op jit(solution)/shard_map/all_to_all | solution.py:87
  731.7 15.1 %copy.352 = bf16[1024,8,640]{0,2,1:T(8,128)(2,1)} copy(bf16[1024,8,640]{2,0,1:T(8,128)(2,1)} %bitcast.24) | data formatting | bytes 20971520 | tf_op jit(solution)/shard_map/all_to_all | solution.py:95
  752.9 6.4 all-to-all-done.13
  792.0 6.3 all-to-all-done.10
  821.0 6.5 all-to-all-done.16
  831.1 6.4 all-to-all-done.12
  841.1 6.4 all-to-all-done.8
  851.1 6.4 all-to-all-done.3
  891.2 7.5 convolution_convert_fusion.3
  898.7 7.5 convolution_convert_fusion.2
  912.0 7.5 convolution_convert_fusion.1
  919.5 7.5 convolution_convert_fusion
  928.2 74.4 %all-reduce.7.cloned.1.call-done = (bf16[16,5120]{1,0:T(8,128)(2,1)}, bf16[16,5120]{1,0:T(8,128)(2,1)}, bf16[16,5120]{1,0:T(8,128)(2,1)}, bf16[16,5120]{1,0:T(8,128)(2,1)}) async-done(((bf16[16,5120]{1,0:T(8,128)(2,1)}, bf16[16,5120]{1,0:T(8,128)(2,1)}, bf16[16,5120]{1,0:T(8,128)(2,1)}, bf16[16,5120]{1,0:T(8,128)(2,1)}), (bf16[16,5120]{1,0:T(8,128)(2,1)}, bf16[16,5120]{1,0:T(8,128)(2,1)}, ...) | async-done | bytes 655376
  (211 shorter events, 182.8 us)
Async XLA Ops:
  6.5 14.5 %all-gather.13.cloned.1.call-start = ((), (), s32[]{:S(2)}) async-start(), calls=%async_computation.22 | async-start | bytes 1966080 | tf_op jit(solution)/shard_map/all_gather | solution.py:84
  7.3 26.0 %all-gather.11.cloned.1.call-start = ((), (), s32[]{:S(2)}) async-start(), calls=%async_computation.21 | async-start | bytes 1966080 | tf_op jit(solution)/shard_map/all_gather | solution.py:83
  8.0 57.4 %all-gather.9.cloned.1.call-start = ((), (), s32[]{:S(2)}) async-start(), calls=%async_computation.20 | async-start | bytes 15728640 | tf_op jit(solution)/shard_map/all_gather | solution.py:82
  23.5 37.6 %all-to-all-start.2 = ((bf16[640,8,128]{0,2,1:T(8,128)(2,1)}), bf16[640,8,128]{0,2,1:T(8,128)(2,1)S(1)}, u32[]{:S(2)}, u32[]{:S(2)}) async-start(bf16[640,8,128]{0,2,1:T(8,128)(2,1)} %bitcast.196), calls=%async_computation.2 | async-start | bytes 2621440 | tf_op jit(solution)/shard_map/all_to_all | solution.py:89
  61.1 35.3 %all-to-all-start.1 = ((bf16[640,8,128]{0,2,1:T(8,128)(2,1)}), bf16[640,8,128]{0,2,1:T(8,128)(2,1)}, u32[]{:S(2)}, u32[]{:S(2)}) async-start(bf16[640,8,128]{0,2,1:T(8,128)(2,1)} %bitcast.195), calls=%async_computation.1 | async-start | bytes 2621440 | tf_op jit(solution)/shard_map/all_to_all | solution.py:88
  96.4 231.9 %all-to-all-start = ((bf16[640,8,1024]{0,2,1:T(8,128)(2,1)}), bf16[640,8,1024]{0,2,1:T(8,128)(2,1)}, u32[]{:S(2)}, u32[]{:S(2)}) async-start(bf16[640,8,1024]{0,2,1:T(8,128)(2,1)} %bitcast.189), calls=%async_computation | async-start | bytes 20971520 | tf_op jit(solution)/shard_map/all_to_all | solution.py:87
  101.6 26.3 %all-gather.15.cloned.1.call-start = ((), (), s32[]{:S(2)}) async-start(), calls=%async_computation.23 | async-start | bytes 15728640 | tf_op jit(solution)/shard_map/all_gather | solution.py:94
  328.3 393.8 %all-to-all-start.7 = ((bf16[8,1024,640]{2,1,0:T(8,128)(2,1)}), bf16[8,1024,640]{2,1,0:T(8,128)(2,1)}, u32[]{:S(2)}, u32[]{:S(2)}) async-start(bf16[8,1024,640]{2,1,0:T(8,128)(2,1)} %bitcast.188), calls=%async_computation.7 | async-start | bytes 20971520 | tf_op jit(solution)/shard_map/all_to_all | solution.py:95
  722.1 24.7 %all-to-all-start.17 = ((bf16[8,2,128]{2,1,0:T(2,128)(2,1)}), bf16[8,2,128]{2,1,0:T(2,128)(2,1)S(1)}, u32[]{:S(2)}, u32[]{:S(2)}) async-start(bf16[8,2,128]{2,1,0:T(2,128)(2,1)} %bitcast.68), calls=%async_computation.17 | async-start | bytes 8192 | tf_op jit(solution)/shard_map/all_to_all | solution.py:114
  746.8 12.5 %all-to-all-start.13 = ((bf16[8,2,128]{2,1,0:T(2,128)(2,1)}), bf16[8,2,128]{2,1,0:T(2,128)(2,1)S(1)}, u32[]{:S(2)}, u32[]{:S(2)}) async-start(bf16[8,2,128]{2,1,0:T(2,128)(2,1)} %bitcast.51), calls=%async_computation.13 | async-start | bytes 8192 | tf_op jit(solution)/shard_map/all_to_all | solution.py:114
  759.2 9.9 all-to-all-start.9
  769.2 9.7 all-to-all-start.4
  778.9 9.7 all-to-all-start.5
  788.6 9.7 all-to-all-start.10
  807.9 9.7 all-to-all-start.18
  817.6 10.0 all-to-all-start.16
  827.6 10.0 all-to-all-start.12
  837.5 10.0 all-to-all-start.8
  847.5 10.0 all-to-all-start.3
  861.9 13.2 %all-to-all-start.6 = ((bf16[2,8,1024]{2,0,1:T(2,128)(2,1)}), bf16[2,8,1024]{2,0,1:T(2,128)(2,1)S(1)}, u32[]{:S(2)}, u32[]{:S(2)}) async-start(bf16[2,8,1024]{2,0,1:T(2,128)(2,1)} %copy.350), calls=%async_computation.6 | async-start | bytes 65536 | tf_op jit(solution)/shard_map/all_to_all | solution.py:135
  875.0 12.6 %all-to-all-start.11 = ((bf16[2,8,1024]{2,0,1:T(2,128)(2,1)}), bf16[2,8,1024]{2,0,1:T(2,128)(2,1)S(1)}, u32[]{:S(2)}, u32[]{:S(2)}) async-start(bf16[2,8,1024]{2,0,1:T(2,128)(2,1)} %copy.362), calls=%async_computation.11 | async-start | bytes 65536 | tf_op jit(solution)/shard_map/all_to_all | solution.py:135
  887.7 18.5 %all-to-all-start.15 = ((bf16[2,8,1024]{2,0,1:T(2,128)(2,1)}), bf16[2,8,1024]{2,0,1:T(2,128)(2,1)S(1)}, u32[]{:S(2)}, u32[]{:S(2)}) async-start(bf16[2,8,1024]{2,0,1:T(2,128)(2,1)} %copy.371), calls=%async_computation.15 | async-start | bytes 65536 | tf_op jit(solution)/shard_map/all_to_all | solution.py:135
  906.2 13.3 %all-to-all-start.19 = ((bf16[2,8,1024]{2,0,1:T(2,128)(2,1)}), bf16[2,8,1024]{2,0,1:T(2,128)(2,1)S(1)}, u32[]{:S(2)}, u32[]{:S(2)}) async-start(bf16[2,8,1024]{2,0,1:T(2,128)(2,1)} %copy.381), calls=%async_computation.19 | async-start | bytes 65536 | tf_op jit(solution)/shard_map/all_to_all | solution.py:135
  911.9 90.8 %all-reduce.7.cloned.1.call-start = ((), (), s32[]{:S(2)}) async-start(), calls=%async_computation.24 | async-start | bytes 1310720
  (19 other events, 1623.8 us)
Sparse Core Ops, SparseCore 0:
  8.9 12.1 all-gather.12
  22.6 10.5 all-gather.10
  34.8 24.0 all-gather.8
  103.7 24.1 all-gather.14
  927.1 75.5 all-reduce.6
where the time goes:
time: 1010 us
  waiting for transfers between devices  422 us (42%)
  blocking collectives  346 us (34%)
  local copies, waits for them, and re-layouts  87 us (9%)
  starting transfers between devices  81.9 us (8%)
  matrix products  53.4 us (5%)
  between operations  14.5 us (1%)
    all_gather x4, blocking collectives, body(): lax.all_gather(normed, 'tensor', axis=0, tiled=True)  346 us
    all_to_all x1, waiting for transfers between devices, body(): lax.all_to_all(relayed[0], 'tensor', split_axis=1, concat_axis=0, tiled=T...  186 us
    unnamed x6, waiting for transfers between devices  77 us
    dot_general x4, matrix products, body(): jnp.dot(head_layout, out_weight, preferred_element_type=jnp.float32)  29.9 us
    all_to_all x4, waiting for transfers between devices, body(): lax.all_to_all(q_part, 'tensor', split_axis=0, concat_axis=1, tiled=True)  25.8 us
    all_gather x1, waiting for transfers between devices, body(): out_weight = lax.all_gather(w_out, 'side', axis=1, tiled=True)  25.7 us
    all_to_all x1, waiting for transfers between devices, body(): lax.all_to_all(relayed[2], 'tensor', split_axis=1, concat_axis=0, tiled=T...  25.5 us
    all_to_all x4, waiting for transfers between devices, body(): lax.all_to_all(v_part, 'tensor', split_axis=0, concat_axis=1, tiled=True)  24.9 us
  transfers between devices with their start and end apart: 25, of which 19 were waited for; matrix products, arithmetic and copies ran while one was open for 13% of the time, Pallas kernels for 0%

commit v1 on v0

v1 whole, which is shorter than its diff:
```python
import jax
import jax.numpy as jnp
from jax import lax
from jax.sharding import PartitionSpec as P

rope_base = 1000000.0
norm_eps = 1e-06
masked_score = -1e30
ring = ("tensor", "side")


def rms_scale(values, gain_vector):
    mean_square = jnp.mean(values * values, axis=-1, keepdims=True)
    return values * lax.rsqrt(mean_square + norm_eps) * gain_vector


def rotate(values, positions):
    half_dim = values.shape[-1] // 2
    frequency = rope_base ** (-2.0 * jnp.arange(half_dim, dtype=jnp.float32) / values.shape[-1])
    angles = positions[..., None] * frequency
    cosine = jnp.cos(angles)[..., None, :]
    sine_part = jnp.sin(angles)[..., None, :]
    lower_half = values[..., :half_dim]
    upper_half = values[..., half_dim:]
    return jnp.concatenate(
        [
            lower_half * cosine - upper_half * sine_part,
            upper_half * cosine + lower_half * sine_part,
        ],
        axis=-1,
    )


def attend(queries, cache_k, cache_v, lengths, fresh_k, fresh_v):
    step_total, row_count, head_count, head_size = queries.shape
    kv_count, context = cache_k.shape[1:3]
    group = head_count // kv_count
    grouped = queries.reshape(step_total, row_count, kv_count, group, head_size)
    grouped = grouped.transpose(1, 2, 0, 3, 4).reshape(
        row_count, kv_count, step_total * group, head_size
    )
    fresh_k = fresh_k.transpose(1, 2, 0, 3)
    fresh_v = fresh_v.transpose(1, 2, 0, 3)
    score_scale = head_size ** (-0.5)
    cached_scores = (
        jnp.einsum("rkqd,rkld->rkql", grouped, cache_k, preferred_element_type=jnp.float32)
        * score_scale
    )
    live_mask = jnp.arange(context, dtype=jnp.int32)[None, :] < lengths[:, None]
    cached_scores = jnp.where(live_mask[:, None, None, :], cached_scores, masked_score)
    fresh_scores = (
        jnp.einsum("rkqd,rksd->rkqs", grouped, fresh_k, preferred_element_type=jnp.float32)
        * score_scale
    )
    query_step = jnp.arange(step_total * group, dtype=jnp.int32) // group
    causal = jnp.arange(step_total, dtype=jnp.int32)[None, :] <= query_step[:, None]
    fresh_scores = jnp.where(causal, fresh_scores, masked_score)
    highest = jnp.maximum(jnp.max(cached_scores, axis=-1), jnp.max(fresh_scores, axis=-1))[
        ..., None
    ]
    cached_exp = jnp.exp(cached_scores - highest)
    fresh_exp = jnp.exp(fresh_scores - highest)
    denominator = jnp.sum(cached_exp, axis=-1, keepdims=True) + jnp.sum(
        fresh_exp, axis=-1, keepdims=True
    )
    cached_weight = (cached_exp / denominator).astype(jnp.bfloat16)
    fresh_weight = (fresh_exp / denominator).astype(jnp.bfloat16)
    mixed_out = jnp.einsum(
        "rkql,rkld->rkqd", cached_weight, cache_v, preferred_element_type=jnp.float32
    )
    mixed_out = mixed_out + jnp.einsum(
        "rkqs,rksd->rkqd", fresh_weight, fresh_v, preferred_element_type=jnp.float32
    )
    mixed_out = mixed_out.astype(jnp.bfloat16)
    mixed_out = mixed_out.reshape(row_count, kv_count, step_total, group, head_size)
    return mixed_out.transpose(2, 0, 1, 3, 4).reshape(
        step_total * row_count, head_count * head_size
    )


def body(
    hidden,
    norm_gain,
    query_gain,
    key_gain,
    w_query,
    w_key,
    w_value,
    w_out,
    cache_k,
    cache_v,
    lengths,
):
    step_total, row_count, model_width = hidden.shape
    own_rows = step_total * row_count
    head_size = query_gain.shape[0]
    query_width, key_width = w_query.shape[1], w_key.shape[1]
    residual = hidden.astype(jnp.float32)
    normed = rms_scale(residual, norm_gain).astype(jnp.bfloat16).reshape(own_rows, model_width)
    slab = lax.all_to_all(normed, ring, split_axis=1, concat_axis=0, tiled=True)
    partial_sums = jnp.concatenate(
        [
            jnp.dot(slab, weight, preferred_element_type=jnp.float32)
            for weight in (w_query, w_key, w_value)
        ],
        axis=1,
    )
    projected = lax.psum_scatter(partial_sums, ring, scatter_dimension=0, tiled=True).astype(
        jnp.bfloat16
    )
    q_heads = projected[:, :query_width].astype(jnp.float32)
    k_heads = projected[:, query_width : query_width + key_width].astype(jnp.float32)
    fresh_v = projected[:, query_width + key_width :]
    positions = lengths.astype(jnp.float32)[None, :] + jnp.arange(step_total, dtype=jnp.float32)[:, None]
    q_heads = q_heads.reshape(step_total, row_count, -1, head_size)
    k_heads = k_heads.reshape(step_total, row_count, -1, head_size)
    queries = rotate(rms_scale(q_heads, query_gain), positions).astype(jnp.bfloat16)
    fresh_k = rotate(rms_scale(k_heads, key_gain), positions).astype(jnp.bfloat16)
    fresh_v = fresh_v.reshape(step_total, row_count, -1, head_size)
    attended = attend(queries, cache_k, cache_v, lengths, fresh_k, fresh_v)
    everyone = lax.all_gather(attended, ring, axis=0, tiled=True)
    columns = jnp.dot(everyone, w_out, preferred_element_type=jnp.float32)
    update = lax.all_to_all(columns, ring, split_axis=0, concat_axis=1, tiled=True)
    update = update.reshape(step_total, row_count, model_width)
    return (residual + update).astype(jnp.bfloat16)


def solution(mesh):
    placed = (
        P(None, ("groups", "tensor", "side"), None),
        P(),
        P(),
        P(),
        P(("tensor", "side"), None),
        P(("tensor", "side"), None),
        P(("tensor", "side"), None),
        P(None, ("tensor", "side")),
        P(("groups", "tensor", "side"), None, None, None),
        P(("groups", "tensor", "side"), None, None, None),
        P(("groups", "tensor", "side")),
    )
    return jax.shard_map(
        body,
        mesh=mesh,
        in_specs=placed,
        out_specs=P(None, ("groups", "tensor", "side"), None),
        check_vma=False,
    )
```

time: 1010 us -> 178 us (0.18)
  blocking collectives: 346 us -> 26.9 us
  waiting for transfers between devices: 422 us -> 116 us
  local copies, waits for them, and re-layouts: 87 us -> 1.87 us
  starting transfers between devices: 81.9 us -> 0.04 us
  matrix products: 53.4 us -> 11.6 us
    all_gather x4 -> x0, blocking collectives: 346 us -> none  [body(): lax.all_gather(normed, 'tensor', axis=0, tiled=True)]
    all_to_all x20 -> x0, waiting for transfers between devices: 303 us -> none  [the longest x1 186 us: body(): lax.all_to_all(relayed[0], 'tensor', split_axis=1, concat_axis=0, tiled=T...]
    all_to_all x20 -> x0, starting transfers between devices: 81.7 us -> none  [the longest x4 18.5 us: body(): lax.all_to_all(attended, 'tensor', split_axis=1, concat_axis=0, tiled=True)]
    unnamed x6 -> x2, waiting for transfers between devices: 77 us -> 0.03 us
    reduce_scatter x0 -> x1, waiting for transfers between devices: none -> 75.1 us  [body(): lax.psum_scatter(partial_sums, ring, scatter_dimension=0, tiled=True)]
    dot_general x23 -> x8, matrix products: 53.4 us -> 11.6 us  [the longest x1 5.1 us: body(): columns = jnp.dot(everyone, w_out, preferred_element_type=jnp.float32)]
    all_to_all x14 -> x3, local copies, waits for them, and re-layouts: 36.8 us -> 0.18 us  [the longest x2 0.14 us: body(): slab = lax.all_to_all(normed, ring, split_axis=1, concat_axis=0, tiled=True)]
    all_gather x4 -> x0, local copies, waits for them, and re-layouts: 33.6 us -> none  [the longest x1 14.4 us: body(): out_weight = lax.all_gather(w_out, 'side', axis=1, tiled=True)]
  transfers between devices with their start and end apart: 25 -> 2, of which waited for: 19 -> 2; matrix products, arithmetic and copies ran while one was open for 13% -> 0% of each run, Pallas kernels for 0% -> 0%
where the time goes in v1:
time: 178 us
  waiting for transfers between devices  116 us (65%)
  blocking collectives  26.9 us (15%)
  between operations  13.7 us (8%)
  matrix products  11.6 us (7%)
  other arithmetic  8.04 us (5%)
  local copies, waits for them, and re-layouts  1.87 us (1%)
    reduce_scatter x1, waiting for transfers between devices, body(): lax.psum_scatter(partial_sums, ring, scatter_dimension=0, tiled=True)  75.1 us
    all_gather x1, waiting for transfers between devices, body(): everyone = lax.all_gather(attended, ring, axis=0, tiled=True)  40.5 us
    all_to_all x1, blocking collectives, body(): slab = lax.all_to_all(normed, ring, split_axis=1, concat_axis=0, tiled=True)  14.6 us
    all_to_all x1, blocking collectives, body(): lax.all_to_all(columns, ring, split_axis=0, concat_axis=1, tiled=True)  12.3 us
    dot_general x1, matrix products, body(): columns = jnp.dot(everyone, w_out, preferred_element_type=jnp.float32)  5.1 us
    dot_general x3, matrix products, body(): jnp.dot(slab, weight, preferred_element_type=jnp.float32)  4.48 us
  transfers between devices with their start and end apart: 2, of which 2 were waited for; matrix products, arithmetic and copies ran while one was open for 0% of the time, Pallas kernels for 0%

profile of v1, /device:TPU:0, one launch (start us, length us, event | category | flops | bytes accessed | tf_op | source)
XLA Modules:
  0.0 177.7 jit_solution(17530321480181570453)
XLA Ops:
  6.5 1.2 fusion.7
  7.8 1.0 fusion.9
  9.0 14.6 %all_to_all.35 = bf16[8,16,320]{2,0,1:T(8,128)(2,1)S(1)} all-to-all(bf16[8,16,320]{2,0,1:T(8,128)(2,1)S(1)} %copy.49), channel_id=1, replica_groups=mesh['groups'=2,'tensor'=8,'side'=2] {'tensor','side'}, dimensions={1} | all-to-all | bytes 163840 | tf_op jit(solution)/shard_map/all_to_all | solution.py:100
  23.6 3.9 %fusion.21 = f32[128,8192]{1,0:T(8,128)S(1)} fusion(bf16[320,8192]{1,0:T(8,128)(2,1)} %param.15, bf16[8,16,320]{2,0,1:T(8,128)(2,1)S(1)} %all_to_all.35), kind=kOutput, calls=%fused_computation.38 | convolution fusion | flops 671088640 | bytes 9519104 | tf_op jit(solution)/shard_map/dot_general | solution.py:103
  27.5 0.3 fusion.17
  27.8 0.3 fusion.19
  28.1 2.7 %pad_maximum_fusion = f32[128,10240]{1,0:T(8,128)} fusion(f32[128,1024]{1,0:T(8,128)S(1)} %fusion.17, f32[128,1024]{1,0:T(8,128)S(1)} %fusion.19, f32[128,8192]{1,0:T(8,128)S(1)} %fusion.21), kind=kLoop, calls=%fused_computation | loop fusion | flops 2621440 | bytes 10485760 | tf_op jit(solution)/shard_map/concatenate | solution.py:101
  30.8 0.6 copy-done.6
  31.8 75.1 %reduce-scatter.2.cloned.1.call-done = f32[8,10240]{1,0:T(8,128)} async-done(((f32[128,10240]{1,0:T(8,128)}), f32[8,10240]{1,0:T(8,128)}) %reduce-scatter.2.cloned.1.call-update) | async-done | bytes 327696 | tf_op jit(solution)/shard_map/reduce_scatter | solution.py:108
  106.8 1.0 convert_element_type.31
  108.3 0.1 multiply_reduce_fusion
  108.5 0.1 multiply_multiply_fusion
  108.7 0.2 fusion.11
  108.8 0.9 fusion.35
  109.8 0.3 fusion.36
  110.1 0.3 fusion.4
  110.4 0.2 fusion.25
  110.7 0.5 fusion.2
  111.3 0.7 reshape.142
  112.0 40.5 %all-gather.2.cloned.1.call-done = bf16[128,8192]{1,0:T(8,128)(2,1)} async-done(((bf16[8,8192]{1,0:T(8,128)(2,1)}), bf16[128,8192]{1,0:T(8,128)(2,1)}) %all-gather.2.cloned.1.call-update) | async-done | bytes 2097168 | tf_op jit(solution)/shard_map/all_gather | solution.py:121
  152.5 5.1 %convolution_bitcast_fusion = f32[16,8,320]{2,1,0:T(8,128)S(1)} fusion(bf16[128,8192]{1,0:T(8,128)(2,1)} %all-gather.2.cloned.1.call-done, bf16[8192,320]{0,1:T(8,128)(2,1)} %param.18), kind=kOutput, calls=%fused_computation.5 | convolution fusion | flops 671088640 | bytes 7503872 | tf_op jit(solution)/shard_map/dot_general | solution.py:122
  157.6 12.3 %all_to_all.36 = f32[16,8,320]{2,1,0:T(8,128)S(1)} all-to-all(f32[16,8,320]{2,1,0:T(8,128)S(1)} %convolution_bitcast_fusion), channel_id=1, replica_groups=mesh['groups'=2,'tensor'=8,'side'=2] {'tensor','side'}, dimensions={0} | all-to-all | bytes 327680 | tf_op jit(solution)/shard_map/all_to_all | solution.py:123
  169.9 0.2 reshape.143
  170.1 0.7 fusion.10
  (47 shorter events, 1.1 us)
Async XLA Ops:
  6.5 102.3 %copy-start = (bf16[2,8,512,128]{3,2,1,0:T(8,128)(2,1)S(1)}, bf16[2,8,512,128]{3,2,1,0:T(8,128)(2,1)}, u32[]{:S(2)}) copy-start(bf16[2,8,512,128]{3,2,1,0:T(8,128)(2,1)} %param.19) | copy-start | bytes 6291460
  6.5 100.3 %reduce-scatter.2.cloned.1.call-start = ((), (), s32[]{:S(2)}) async-start(), calls=%async_computation.3 | async-start | bytes 5570560 | tf_op jit(solution)/shard_map/reduce_scatter | solution.py:108
  23.6 3.9 %copy-start.2 = (bf16[320,1024]{1,0:T(8,128)(2,1)S(1)}, bf16[320,1024]{1,0:T(8,128)(2,1)}, u32[]{:S(2)}) copy-start(bf16[320,1024]{1,0:T(8,128)(2,1)} %param.17) | copy-start | bytes 1966084
  23.6 4.2 %copy-start.3 = (bf16[320,1024]{1,0:T(8,128)(2,1)S(1)}, bf16[320,1024]{1,0:T(8,128)(2,1)}, u32[]{:S(2)}) copy-start(bf16[320,1024]{1,0:T(8,128)(2,1)} %param.16) | copy-start | bytes 1966084
  30.8 0.7 copy-start.6
  30.8 77.3 %copy-start.4 = (f32[128]{0:T(128)S(1)}, f32[128]{0:T(128)}, u32[]{:S(2)}) copy-start(f32[128]{0:T(128)} %param.14) | copy-start | bytes 1540
  30.8 77.7 %copy-start.5 = (f32[128]{0:T(128)S(1)}, f32[128]{0:T(128)}, u32[]{:S(2)}) copy-start(f32[128]{0:T(128)} %param.13) | copy-start | bytes 1540
  30.8 121.7 %all-gather.2.cloned.1.call-start = ((), (), s32[]{:S(2)}) async-start(), calls=%async_computation.4 | async-start | bytes 2228224 | tf_op jit(solution)/shard_map/all_gather | solution.py:121
  108.1 2.6 %copy-start.7 = (bf16[2,8,512,128]{3,2,1,0:T(8,128)(2,1)S(1)}, bf16[2,8,512,128]{3,2,1,0:T(8,128)(2,1)}, u32[]{:S(2)}) copy-start(bf16[2,8,512,128]{3,2,1,0:T(8,128)(2,1)} %param.20) | copy-start | bytes 6291460
  112.0 58.1 %copy-start.1 = (bf16[4,2,5120]{2,1,0:T(2,128)(2,1)S(1)}, bf16[4,2,5120]{2,1,0:T(2,128)(2,1)}, u32[]{:S(2)}) copy-start(bf16[4,2,5120]{2,1,0:T(2,128)(2,1)} %param.11) | copy-start | bytes 245764
Sparse Core Ops, SparseCore 0:
  30.9 75.8 reduce-scatter.1
  112.1 40.3 all-gather.1

commit v2 on v1

--- a/solution.py
+++ b/solution.py
@@ -1,6 +1,10 @@
+import functools
+
 import jax
 import jax.numpy as jnp
 from jax import lax
+from jax.experimental import pallas as pl
+from jax.experimental.pallas import tpu as pltpu
 from jax.sharding import PartitionSpec as P
 
 rope_base = 1000000.0
@@ -78,7 +82,366 @@
     )
 
 
+LONG, SHORT, SIDE = 4, 2, 2
+OWNERS = LONG * SHORT * SIDE
+VMEM_BYTES = 56 * 1024 * 1024
+
+
+def place():
+    tensor_index = lax.axis_index("tensor")
+    return tensor_index // SHORT, lax.rem(tensor_index, SHORT), lax.axis_index("side")
+
+
+def others():
+    return [
+        (a, b, c)
+        for a in range(LONG)
+        for b in range(SHORT)
+        for c in range(SIDE)
+        if (a, b, c) != (0, 0, 0)
+    ]
+
+
+def slot(step):
+    a, b, c = step
+    return (a * SHORT + b) * SIDE + c
+
+
+def shifted(me, step):
+    return tuple(
+        lax.rem(i + d, n) for i, d, n in zip(me, step, (LONG, SHORT, SIDE), strict=True)
+    )
+
+
+def device(where):
+    return {"tensor": where[0] * SHORT + where[1], "side": where[2]}
+
+
+def number(where):
+    return (where[0] * SHORT + where[1]) * SIDE + where[2]
+
+
+def by_side(where):
+    return (where[2] * SHORT + where[1]) * LONG + where[0]
+
+
+def remote(src, dst, send_sem, recv_sem, where):
+    return pltpu.make_async_remote_copy(
+        src_ref=src,
+        dst_ref=dst,
+        send_sem=send_sem,
+        recv_sem=recv_sem,
+        device_id=device(where),
+        device_id_type=pl.DeviceIdType.MESH,
+    )
+
+
+def greet(me):
+    barrier = pltpu.get_barrier_semaphore()
+    for step in others():
+        pl.semaphore_signal(
+            barrier,
+            inc=1,
+            device_id=device(shifted(me, step)),
+            device_id_type=pl.DeviceIdType.MESH,
+        )
+    pl.semaphore_wait(barrier, OWNERS - 1)
+
+
+def project_kernel(
+    width,
+    x_ref,
+    wq_ref,
+    wk_ref,
+    wv_ref,
+    out_ref,
+    wq,
+    wk,
+    wv,
+    slab,
+    first,
+    from_side,
+    second,
+    from_short,
+    third,
+    from_long,
+    load_sem,
+    slab_send,
+    slab_recv,
+    send_sem,
+    recv_sem,
+):
+    me = place()
+    long_index, short_index, side_index = me
+    loads = [
+        pltpu.make_async_copy(src, dst, load_sem.at[i])
+        for i, (src, dst) in enumerate(((wq_ref, wq), (wk_ref, wk), (wv_ref, wv)))
+    ]
+    for load in loads:
+        load.start()
+    greet(me)
+    scattered = []
+    for step in others():
+        target = shifted(me, step)
+        copy = remote(
+            x_ref.at[number(target)],
+            slab.at[by_side(me)],
+            slab_send.at[slot(step)],
+            slab_recv.at[slot(step)],
+            target,
+        )
+        copy.start()
+        scattered.append(copy)
+    slab[by_side(me)] = x_ref[number(me)]
+    for load in loads:
+        load.wait()
+    for copy in scattered:
+        copy.wait_recv()
+    own_rows, depth = slab.shape[1:]
+    left = slab[...].reshape(OWNERS * own_rows, depth).astype(jnp.bfloat16)
+
+    pieces = []
+    for weight in (wq, wk, wv):
+        pieces += [(weight, start) for start in range(0, weight.shape[1], width)]
+    total = len(pieces)
+    sent = []
+
+    def multiply(c):
+        weight, start = pieces[c]
+        product = jnp.dot(
+            left, weight[:, start : start + width], preferred_element_type=jnp.float32
+        )
+        first[c] = product.reshape(SIDE, SHORT, LONG, own_rows, width)
+        copy = remote(
+            first.at[c, 1 - side_index],
+            from_side.at[c],
+            send_sem.at[c, 0],
+            recv_sem.at[c, 0],
+            shifted(me, (0, 0, 1)),
+        )
+        copy.start()
+        sent.append(copy)
+        return copy
+
+    def add_side(c, arrived):
+        arrived.wait_recv()
+        second[c] = first[c, side_index] + from_side[c]
+        copy = remote(
+            second.at[c, 1 - short_index],
+            from_short.at[c],
+            send_sem.at[c, 1],
+            recv_sem.at[c, 1],
+            shifted(me, (0, 1, 0)),
+        )
+        copy.start()
+        sent.append(copy)
+        return copy
+
+    def add_short(c, arrived):
+        arrived.wait_recv()
+        third[c] = second[c, short_index] + from_short[c]
+        copies = []
+        for hop in range(1, LONG):
+            target = shifted(me, (hop, 0, 0))
+            copy = remote(
+                third.at[c, target[0]],
+                from_long.at[c, hop - 1],
+                send_sem.at[c, 1 + hop],
+                recv_sem.at[c, 1 + hop],
+                target,
+            )
+            copy.start()
+            copies.append(copy)
+        sent.extend(copies)
+        return copies
+
+    def add_long(c, arrived):
+        value = third[c, long_index]
+        for hop, copy in enumerate(arrived):
+            copy.wait_recv()
+            value = value + from_long[c, hop]
+        out_ref[:, c * width : (c + 1) * width] = value
+
+    side_copies = [None] * total
+    short_copies = [None] * total
+    long_copies = [None] * total
+    for tick in range(total + 4):
+        if tick < total:
+            side_copies[tick] = multiply(tick)
+        if 0 <= tick - 1 < total:
+            short_copies[tick - 1] = add_side(tick - 1, side_copies[tick - 1])
+        if 0 <= tick - 3 < total:
+            long_copies[tick - 3] = add_short(tick - 3, short_copies[tick - 3])
+        if 0 <= tick - 4 < total:
+            add_long(tick - 4, long_copies[tick - 4])
+    for copy in scattered + sent:
+        copy.wait_send()
+
+
+def project(blocks, w_query, w_key, w_value):
+    own_rows, depth = blocks.shape[1:]
+    width = w_key.shape[1]
+    columns = w_query.shape[1] + w_key.shape[1] + w_value.shape[1]
+    total = columns // width
+    f32 = jnp.float32
+    hbm = pl.BlockSpec(memory_space=pl.ANY)
+    vmem = pl.BlockSpec(memory_space=pltpu.VMEM)
+    return pl.pallas_call(
+        functools.partial(project_kernel, width),
+        out_shape=jax.ShapeDtypeStruct((own_rows, columns), f32),
+        in_specs=[vmem, hbm, hbm, hbm],
+        out_specs=vmem,
+        scratch_shapes=[
+            pltpu.VMEM(w_query.shape, w_query.dtype),
+            pltpu.VMEM(w_key.shape, w_key.dtype),
+            pltpu.VMEM(w_value.shape, w_value.dtype),
+            pltpu.VMEM(blocks.shape, f32),
+            pltpu.VMEM((total, SIDE, SHORT, LONG, own_rows, width), f32),
+            pltpu.VMEM((total, SHORT, LONG, own_rows, width), f32),
+            pltpu.VMEM((total, SHORT, LONG, own_rows, width), f32),
+            pltpu.VMEM((total, LONG, own_rows, width), f32),
+            pltpu.VMEM((total, LONG, own_rows, width), f32),
+            pltpu.VMEM((total, LONG - 1, own_rows, width), f32),
+            pltpu.SemaphoreType.DMA((3,)),
+            pltpu.SemaphoreType.DMA((OWNERS,)),
+            pltpu.SemaphoreType.DMA((OWNERS,)),
+            pltpu.SemaphoreType.DMA((total, 1 + LONG)),
+            pltpu.SemaphoreType.DMA((total, 1 + LONG)),
+        ],
+        compiler_params=pltpu.CompilerParams(
+            collective_id=0, has_side_effects=True, vmem_limit_bytes=VMEM_BYTES
+        ),
+    )(blocks, w_query, w_key, w_value)
+
+
+def output_kernel(
+    tile,
+    x_ref,
+    w_ref,
+    out_ref,
+    weight,
+    gathered,
+    low,
+    high,
+    result,
+    load_sem,
+    own_sem,
+    send_sem,
+    recv_sem,
+    back_send,
+    back_recv,
+):
+    me = place()
+    load = pltpu.make_async_copy(w_ref, weight, load_sem)
+    load.start()
+    own = pltpu.make_async_copy(x_ref, gathered.at[number(me)], own_sem)
+    own.start()
+    greet(me)
+    own.wait()
+    copies = {}
+
+    def pass_on(origin_step, step):
+        behind = tuple((n - d) % n for d, n in zip(origin_step, (LONG, SHORT, SIDE)))
+        block = gathered.at[number(shifted(me, behind))]
+        arrival = tuple(o + d for o, d in zip(origin_step, step))
+        copy = remote(
+            block,
+            block,
+            send_sem.at[slot(arrival)],
+            recv_sem.at[slot(arrival)],
+            shifted(me, step),
+        )
+        copy.start()
+        copies[arrival] = copy
+
+    for hop in (2, 1, 3):
+        pass_on((0, 0, 0), (hop, 0, 0))
+    pass_on((0, 0, 0), (0, 1, 0))
+    pass_on((0, 0, 0), (0, 0, 1))
+    for hop in (1, 3, 2):
+        copies[(hop, 0, 0)].wait_recv()
+        pass_on((hop, 0, 0), (0, 1, 0))
+        pass_on((hop, 0, 0), (0, 0, 1))
+    for hop in (0, 1, 3, 2):
+        copies[(hop, 1, 0)].wait_recv()
+        pass_on((hop, 1, 0), (0, 0, 1))
+    for hop in range(LONG):
+        for short in range(SHORT):
+            copies[(hop, short, 1)].wait_recv()
+    load.wait()
+
+    owners, block_rows, half = gathered.shape
+    low[...] = jnp.zeros_like(low)
+    high[...] = jnp.zeros_like(high)
+
+    @pl.loop(0, half // tile)
+    def _(index):
+        start = pl.multiple_of(index * tile, tile)
+        left = gathered[:, :, pl.ds(start, tile)].reshape(owners * block_rows, tile)
+        upper = pl.multiple_of(half + index * tile, tile)
+        low[...] += jnp.dot(
+            left, weight[pl.ds(start, tile), :], preferred_element_type=jnp.float32
+        )
+        high[...] += jnp.dot(
+            left, weight[pl.ds(upper, tile), :], preferred_element_type=jnp.float32
+        )
+
+    own_rows = block_rows // 2
+    wide = (owners, block_rows, low.shape[1])
+    result[...] = (
+        low[...].reshape(wide)[:, :own_rows] + high[...].reshape(wide)[:, own_rows:]
+    )
+    returned = []
+    for step in others():
+        target = shifted(me, step)
+        copy = remote(
+            result.at[number(target)],
+            out_ref.at[number(me)],
+            back_send.at[slot(step)],
+            back_recv.at[slot(step)],
+            target,
+        )
+        copy.start()
+        returned.append(copy)
+    out_ref[number(me)] = result[number(me)]
+    for copy in returned:
+        copy.wait_recv()
+    for copy in list(copies.values()) + returned:
+        copy.wait_send()
+
+
+def output(block, w_out):
+    block_rows, half = block.shape
+    columns = w_out.shape[1]
+    tile = half // 8
+    f32 = jnp.float32
+    vmem = pl.BlockSpec(memory_space=pltpu.VMEM)
+    return pl.pallas_call(
+        functools.partial(output_kernel, tile),
+        out_shape=jax.ShapeDtypeStruct((OWNERS, block_rows // 2, columns), f32),
+        in_specs=[vmem, pl.BlockSpec(memory_space=pl.ANY)],
+        out_specs=vmem,
+        scratch_shapes=[
+            pltpu.VMEM(w_out.shape, w_out.dtype),
+            pltpu.VMEM((OWNERS, block_rows, half), block.dtype),
+            pltpu.VMEM((OWNERS * block_rows, columns), f32),
+            pltpu.VMEM((OWNERS * block_rows, columns), f32),
+            pltpu.VMEM((OWNERS, block_rows // 2, columns), f32),
+            pltpu.SemaphoreType.DMA,
+            pltpu.SemaphoreType.DMA,
+            pltpu.SemaphoreType.DMA((OWNERS,)),
+            pltpu.SemaphoreType.DMA((OWNERS,)),
+            pltpu.SemaphoreType.DMA((OWNERS,)),
+            pltpu.SemaphoreType.DMA((OWNERS,)),
+        ],
+        compiler_params=pltpu.CompilerParams(
+            collective_id=1, has_side_effects=True, vmem_limit_bytes=VMEM_BYTES
+        ),
+    )(block, w_out)
+
+
 def body(
+    direct,
     hidden,
     norm_gain,
     query_gain,
@@ -97,17 +460,20 @@
     query_width, key_width = w_query.shape[1], w_key.shape[1]
     residual = hidden.astype(jnp.float32)
     normed = rms_scale(residual, norm_gain).astype(jnp.bfloat16).reshape(own_rows, model_width)
-    slab = lax.all_to_all(normed, ring, split_axis=1, concat_axis=0, tiled=True)
-    partial_sums = jnp.concatenate(
-        [
-            jnp.dot(slab, weight, preferred_element_type=jnp.float32)
-            for weight in (w_query, w_key, w_value)
-        ],
-        axis=1,
-    )
-    projected = lax.psum_scatter(partial_sums, ring, scatter_dimension=0, tiled=True).astype(
-        jnp.bfloat16
-    )
+    if direct:
+        blocks = normed.astype(jnp.float32).reshape(own_rows, OWNERS, -1).transpose(1, 0, 2)
+        projected = project(blocks, w_query, w_key, w_value)
+    else:
+        slab = lax.all_to_all(normed, ring, split_axis=1, concat_axis=0, tiled=True)
+        partial_sums = jnp.concatenate(
+            [
+                jnp.dot(slab, weight, preferred_element_type=jnp.float32)
+                for weight in (w_query, w_key, w_value)
+            ],
+            axis=1,
+        )
+        projected = lax.psum_scatter(partial_sums, ring, scatter_dimension=0, tiled=True)
+    projected = projected.astype(jnp.bfloat16)
     q_heads = projected[:, :query_width].astype(jnp.float32)
     k_heads = projected[:, query_width : query_width + key_width].astype(jnp.float32)
     fresh_v = projected[:, query_width + key_width :]
@@ -118,9 +484,13 @@
     fresh_k = rotate(rms_scale(k_heads, key_gain), positions).astype(jnp.bfloat16)
     fresh_v = fresh_v.reshape(step_total, row_count, -1, head_size)
     attended = attend(queries, cache_k, cache_v, lengths, fresh_k, fresh_v)
-    everyone = lax.all_gather(attended, ring, axis=0, tiled=True)
-    columns = jnp.dot(everyone, w_out, preferred_element_type=jnp.float32)
-    update = lax.all_to_all(columns, ring, split_axis=0, concat_axis=1, tiled=True)
+    if direct:
+        halves = attended.reshape(own_rows, 2, -1).transpose(1, 0, 2).reshape(2 * own_rows, -1)
+        update = output(halves, w_out).transpose(1, 0, 2)
+    else:
+        everyone = lax.all_gather(attended, ring, axis=0, tiled=True)
+        columns = jnp.dot(everyone, w_out, preferred_element_type=jnp.float32)
+        update = lax.all_to_all(columns, ring, split_axis=0, concat_axis=1, tiled=True)
     update = update.reshape(step_total, row_count, model_width)
     return (residual + update).astype(jnp.bfloat16)
 
@@ -139,8 +509,9 @@
         P(("groups", "tensor", "side"), None, None, None),
         P(("groups", "tensor", "side")),
     )
+    direct = mesh.shape["tensor"] == LONG * SHORT and mesh.shape["side"] == SIDE
     return jax.shard_map(
-        body,
+        functools.partial(body, direct),
         mesh=mesh,
         in_specs=placed,
         out_specs=P(None, ("groups", "tensor", "side"), None),

time: 178 us -> 108 us (0.61)
  waiting for transfers between devices: 116 us -> 0 us
  Pallas kernels: 0 us -> 87.1 us
  blocking collectives: 26.9 us -> 0 us
  between operations: 13.7 us -> 0.24 us
  matrix products: 11.6 us -> 1.97 us
  local copies, waits for them, and re-layouts: 1.87 us -> 11.2 us
    pallas_call x0 -> x2, Pallas kernels: none -> 87.1 us  [the longest x1 51.3 us: project(): pl.pallas_call(functools.partial(project_kernel, width), out_shape=jax.Sh...]
    reduce_scatter x1 -> x0, waiting for transfers between devices: 75.1 us -> none  [body(): lax.psum_scatter(partial_sums, ring, scatter_dimension=0, tiled=True)]
    all_gather x1 -> x0, waiting for transfers between devices: 40.5 us -> none  [body(): everyone = lax.all_gather(attended, ring, axis=0, tiled=True)]
    all_to_all x2 -> x0, blocking collectives: 26.9 us -> none  [the longest x1 14.6 us: body(): slab = lax.all_to_all(normed, ring, split_axis=1, concat_axis=0, tiled=True)]
    dot_general x4 -> x0, matrix products: 9.58 us -> none  [the longest x1 5.1 us: body(): columns = jnp.dot(everyone, w_out, preferred_element_type=jnp.float32)]
    unnamed x19 -> x14, local copies, waits for them, and re-layouts: 0.67 us -> 8.28 us
    concatenate x1 -> x0, other arithmetic: 2.67 us -> none  [body(): jnp.concatenate([jnp.dot(slab, weight, preferred_element_type=jnp.float32...]
    transpose x0 -> x4, local copies, waits for them, and re-layouts: none -> 2.57 us  [the longest x1 0.97 us: body(): update = output(halves, w_out).transpose(1, 0, 2)]
  transfers between devices with their start and end apart: 2 -> 0, of which waited for: 2 -> 0; matrix products, arithmetic and copies ran while one was open for 0% -> 0% of each run, Pallas kernels for 0% -> 0%
where the time goes in v2:
time: 108 us; the launch traced here: 107 us
  Pallas kernels  87.1 us (81%)
  local copies, waits for them, and re-layouts  11.2 us (10%)
  other arithmetic  6.67 us (6%)
  matrix products  1.97 us (2%)
    pallas_call x1, Pallas kernels, project(): pl.pallas_call(functools.partial(project_kernel, width), out_shape=jax.Sh...  51.3 us
    pallas_call x1, Pallas kernels, output(): pl.pallas_call(functools.partial(output_kernel, tile), out_shape=jax.Shap...  35.8 us
    unnamed x14, local copies, waits for them, and re-layouts  8.28 us

profile of v2, /device:TPU:0, one launch (start us, length us, event | category | flops | bytes accessed | tf_op | source)
XLA Modules:
  0.0 107.2 jit_solution(9491379158920845211)
XLA Ops:
  0.0 0.8 convert_element_type.38
  0.9 0.7 iota_compare_fusion
  1.6 1.1 fusion.7
  2.7 0.1 multiply_cosine_fusion
  2.9 1.0 fusion.17
  3.9 0.1 reshape.144
  4.0 0.7 copy.86
  4.8 51.3 %shard_map.109 = f32[8,10240]{1,0:T(8,128)} custom-call(f32[16,8,320]{2,1,0:T(8,128)} %bitcast.54, bf16[320,8192]{1,0:T(8,128)(2,1)} %wq_ref.1, bf16[320,1024]{1,0:T(8,128)(2,1)} %wk_ref.1, bf16[320,1024]{1,0:T(8,128)(2,1)} %wv_ref.1), custom_call_target="tpu_custom_call" | custom-call | tf_op jit(solution)/shard_map/pallas_call | solution.py:289
  56.1 1.0 convert_element_type.37
  57.3 0.1 copy.48
  57.7 0.1 multiply_reduce_fusion
  57.8 0.1 multiply_multiply_fusion
  58.0 0.1 fusion.11
  58.1 0.3 fusion.31
  58.4 0.9 fusion.30
  59.4 0.3 fusion.4
  59.8 0.2 fusion.20
  60.0 0.5 fusion.2
  60.6 0.7 copy.87
  61.3 8.2 %copy.53.w_ref = bf16[8192,320]{1,0:T(8,128)(2,1)} copy(bf16[8192,320]{0,1:T(8,128)(2,1)} %param.18) | data formatting | bytes 10485760 | tf_op args[7]
  69.5 35.8 %shard_map.110 = f32[16,8,320]{2,1,0:T(8,128)} custom-call(bf16[16,4096]{1,0:T(8,128)(2,1)} %bitcast.56, bf16[8192,320]{1,0:T(8,128)(2,1)} %copy.53.w_ref), custom_call_target="tpu_custom_call" | custom-call | tf_op jit(solution)/shard_map/pallas_call | solution.py:419
  105.3 1.0 copy.54
  106.3 0.2 reshape.139
  106.5 0.7 fusion.10
  (32 shorter events, 0.6 us)
Async XLA Ops:
  0.0 58.4 %copy-start = (bf16[2,8,512,128]{3,2,1,0:T(8,128)(2,1)S(1)}, bf16[2,8,512,128]{3,2,1,0:T(8,128)(2,1)}, u32[]{:S(2)}) copy-start(bf16[2,8,512,128]{3,2,1,0:T(8,128)(2,1)} %param.19) | copy-start | bytes 6291460
  4.8 52.6 %copy-start.2 = (f32[128]{0:T(128)S(1)}, f32[128]{0:T(128)}, u32[]{:S(2)}) copy-start(f32[128]{0:T(128)} %param.14) | copy-start | bytes 1540
  56.1 1.7 %copy-start.3 = (f32[128]{0:T(128)S(1)}, f32[128]{0:T(128)}, u32[]{:S(2)}) copy-start(f32[128]{0:T(128)} %param.13) | copy-start | bytes 1540
  58.4 1.6 %copy-start.4 = (bf16[2,8,512,128]{3,2,1,0:T(8,128)(2,1)S(1)}, bf16[2,8,512,128]{3,2,1,0:T(8,128)(2,1)}, u32[]{:S(2)}) copy-start(bf16[2,8,512,128]{3,2,1,0:T(8,128)(2,1)} %param.20) | copy-start | bytes 6291460
  69.5 36.9 %copy-start.1 = (bf16[4,2,5120]{2,1,0:T(2,128)(2,1)S(1)}, bf16[4,2,5120]{2,1,0:T(2,128)(2,1)}, u32[]{:S(2)}) copy-start(bf16[4,2,5120]{2,1,0:T(2,128)(2,1)} %param.11) | copy-start | bytes 245764

commit v3 on v2

--- a/solution.py
+++ b/solution.py
@@ -84,6 +84,7 @@
 
 LONG, SHORT, SIDE = 4, 2, 2
 OWNERS = LONG * SHORT * SIDE
+PIECES = 4
 VMEM_BYTES = 56 * 1024 * 1024
 
 
@@ -265,15 +266,15 @@
     side_copies = [None] * total
     short_copies = [None] * total
     long_copies = [None] * total
-    for tick in range(total + 4):
+    for tick in range(total + 6):
         if tick < total:
             side_copies[tick] = multiply(tick)
         if 0 <= tick - 1 < total:
             short_copies[tick - 1] = add_side(tick - 1, side_copies[tick - 1])
         if 0 <= tick - 3 < total:
             long_copies[tick - 3] = add_short(tick - 3, short_copies[tick - 3])
-        if 0 <= tick - 4 < total:
-            add_long(tick - 4, long_copies[tick - 4])
+        if 0 <= tick - 6 < total:
+            add_long(tick - 6, long_copies[tick - 6])
     for copy in scattered + sent:
         copy.wait_send()
 
@@ -315,7 +316,6 @@
 
 
 def output_kernel(
-    tile,
     x_ref,
     w_ref,
     out_ref,
@@ -332,59 +332,76 @@
     back_recv,
 ):
     me = place()
+    pieces, owners, block_rows, width = gathered.shape
     load = pltpu.make_async_copy(w_ref, weight, load_sem)
     load.start()
-    own = pltpu.make_async_copy(x_ref, gathered.at[number(me)], own_sem)
-    own.start()
+    own = [
+        pltpu.make_async_copy(x_ref.at[p], gathered.at[p, number(me)], own_sem.at[p])
+        for p in range(pieces)
+    ]
+    for copy in own:
+        copy.start()
     greet(me)
-    own.wait()
+    for copy in own:
+        copy.wait()
     copies = {}
 
-    def pass_on(origin_step, step):
+    def pass_on(p, origin_step, step):
         behind = tuple((n - d) % n for d, n in zip(origin_step, (LONG, SHORT, SIDE)))
-        block = gathered.at[number(shifted(me, behind))]
+        block = gathered.at[p, number(shifted(me, behind))]
         arrival = tuple(o + d for o, d in zip(origin_step, step))
         copy = remote(
             block,
             block,
-            send_sem.at[slot(arrival)],
-            recv_sem.at[slot(arrival)],
+            send_sem.at[p, slot(arrival)],
+            recv_sem.at[p, slot(arrival)],
             shifted(me, step),
         )
         copy.start()
-        copies[arrival] = copy
-
-    for hop in (2, 1, 3):
-        pass_on((0, 0, 0), (hop, 0, 0))
-    pass_on((0, 0, 0), (0, 1, 0))
-    pass_on((0, 0, 0), (0, 0, 1))
-    for hop in (1, 3, 2):
-        copies[(hop, 0, 0)].wait_recv()
-        pass_on((hop, 0, 0), (0, 1, 0))
-        pass_on((hop, 0, 0), (0, 0, 1))
-    for hop in (0, 1, 3, 2):
-        copies[(hop, 1, 0)].wait_recv()
-        pass_on((hop, 1, 0), (0, 0, 1))
-    for hop in range(LONG):
-        for short in range(SHORT):
-            copies[(hop, short, 1)].wait_recv()
-    load.wait()
-
-    owners, block_rows, half = gathered.shape
-    low[...] = jnp.zeros_like(low)
-    high[...] = jnp.zeros_like(high)
-
-    @pl.loop(0, half // tile)
-    def _(index):
-        start = pl.multiple_of(index * tile, tile)
-        left = gathered[:, :, pl.ds(start, tile)].reshape(owners * block_rows, tile)
-        upper = pl.multiple_of(half + index * tile, tile)
-        low[...] += jnp.dot(
-            left, weight[pl.ds(start, tile), :], preferred_element_type=jnp.float32
-        )
-        high[...] += jnp.dot(
-            left, weight[pl.ds(upper, tile), :], preferred_element_type=jnp.float32
-        )
+        copies[p, arrival] = copy
+
+    def start_own(p):
+        for hop in (2, 1, 3):
+            pass_on(p, (0, 0, 0), (hop, 0, 0))
+        pass_on(p, (0, 0, 0), (0, 1, 0))
+        pass_on(p, (0, 0, 0), (0, 0, 1))
+
+    def pass_long(p):
+        for hop in (1, 3, 2):
+            copies[p, (hop, 0, 0)].wait_recv()
+            pass_on(p, (hop, 0, 0), (0, 1, 0))
+            pass_on(p, (hop, 0, 0), (0, 0, 1))
+
+    def pass_short(p):
+        for hop in (0, 1, 3, 2):
+            copies[p, (hop, 1, 0)].wait_recv()
+            pass_on(p, (hop, 1, 0), (0, 0, 1))
+
+    def multiply(p):
+        for hop in range(LONG):
+            for short in range(SHORT):
+                copies[p, (hop, short, 1)].wait_recv()
+        left = gathered[p].reshape(owners * block_rows, width)
+        for total, start in ((low, p * width), (high, (pieces + p) * width)):
+            product = lax.dot_general(
+                left,
+                weight[:, start : start + width],
+                (((1,), (1,)), ((), ())),
+                preferred_element_type=jnp.float32,
+            )
+            total[...] = product if p == 0 else total[...] + product
+
+    for p in range(pieces):
+        start_own(p)
+    for tick in range(pieces + 2):
+        if tick < pieces:
+            pass_long(tick)
+        if 0 <= tick - 1 < pieces:
+            pass_short(tick - 1)
+        if tick == 2:
+            load.wait()
+        if 0 <= tick - 2 < pieces:
+            multiply(tick - 2)
 
     own_rows = block_rows // 2
     wide = (owners, block_rows, low.shape[1])
@@ -411,33 +428,32 @@
 
 
 def output(block, w_out):
-    block_rows, half = block.shape
+    pieces, block_rows, width = block.shape
     columns = w_out.shape[1]
-    tile = half // 8
     f32 = jnp.float32
     vmem = pl.BlockSpec(memory_space=pltpu.VMEM)
     return pl.pallas_call(
-        functools.partial(output_kernel, tile),
+        output_kernel,
         out_shape=jax.ShapeDtypeStruct((OWNERS, block_rows // 2, columns), f32),
         in_specs=[vmem, pl.BlockSpec(memory_space=pl.ANY)],
         out_specs=vmem,
         scratch_shapes=[
-            pltpu.VMEM(w_out.shape, w_out.dtype),
-            pltpu.VMEM((OWNERS, block_rows, half), block.dtype),
+            pltpu.VMEM((columns, w_out.shape[0]), w_out.dtype),
+            pltpu.VMEM((pieces, OWNERS, block_rows, width), block.dtype),
             pltpu.VMEM((OWNERS * block_rows, columns), f32),
             pltpu.VMEM((OWNERS * block_rows, columns), f32),
             pltpu.VMEM((OWNERS, block_rows // 2, columns), f32),
             pltpu.SemaphoreType.DMA,
-            pltpu.SemaphoreType.DMA,
-            pltpu.SemaphoreType.DMA((OWNERS,)),
-            pltpu.SemaphoreType.DMA((OWNERS,)),
+            pltpu.SemaphoreType.DMA((pieces,)),
+            pltpu.SemaphoreType.DMA((pieces, OWNERS)),
+            pltpu.SemaphoreType.DMA((pieces, OWNERS)),
             pltpu.SemaphoreType.DMA((OWNERS,)),
             pltpu.SemaphoreType.DMA((OWNERS,)),
         ],
         compiler_params=pltpu.CompilerParams(
             collective_id=1, has_side_effects=True, vmem_limit_bytes=VMEM_BYTES
         ),
-    )(block, w_out)
+    )(block, w_out.T)
 
 
 def body(
@@ -485,7 +501,8 @@
     fresh_v = fresh_v.reshape(step_total, row_count, -1, head_size)
     attended = attend(queries, cache_k, cache_v, lengths, fresh_k, fresh_v)
     if direct:
-        halves = attended.reshape(own_rows, 2, -1).transpose(1, 0, 2).reshape(2 * own_rows, -1)
+        halves = attended.reshape(own_rows, 2, PIECES, -1).transpose(2, 1, 0, 3)
+        halves = halves.reshape(PIECES, 2 * own_rows, -1)
         update = output(halves, w_out).transpose(1, 0, 2)
     else:
         everyone = lax.all_gather(attended, ring, axis=0, tiled=True)

time: 108 us -> 94 us (0.87)
  local copies, waits for them, and re-layouts: 11.2 us -> 2.95 us
  Pallas kernels: 87.1 us -> 81.8 us
    unnamed x14 -> x13, local copies, waits for them, and re-layouts: 8.28 us -> 0.09 us
    pallas_call x1, Pallas kernels: 35.8 us -> 30.5 us  [output(): pl.pallas_call(output_kernel, out_shape=jax.ShapeDtypeStruct((OWNERS, blo...]
where the time goes in v3:
time: 94 us; the launch traced here: 93.7 us
  Pallas kernels  81.8 us (87%)
  other arithmetic  6.67 us (7%)
  local copies, waits for them, and re-layouts  2.95 us (3%)
  matrix products  1.97 us (2%)
    pallas_call x1, Pallas kernels, project(): pl.pallas_call(functools.partial(project_kernel, width), out_shape=jax.Sh...  51.3 us
    pallas_call x1, Pallas kernels, output(): pl.pallas_call(output_kernel, out_shape=jax.ShapeDtypeStruct((OWNERS, blo...  30.5 us

profile of v3, /device:TPU:0, one launch (start us, length us, event | category | flops | bytes accessed | tf_op | source)
XLA Modules:
  0.0 93.7 jit_solution(12958102881153575470)
XLA Ops:
  0.0 0.8 convert_element_type.38
  0.9 0.7 iota_compare_fusion
  1.6 1.1 %fusion.7 = f32[4,2]{1,0:T(4,128)S(1)} fusion(bf16[4,2,5120]{2,1,0:T(2,128)(2,1)} %param.11), kind=kLoop, calls=%fused_computation.21 | loop fusion | flops 122872 | bytes 81952 | tf_op jit(solution)/shard_map/reduce_sum | solution.py:17
  2.7 0.1 multiply_cosine_fusion
  2.9 1.0 %fusion.17 = f32[4,2,5120]{2,1,0:T(2,128)S(1)} fusion(bf16[4,2,5120]{2,1,0:T(2,128)(2,1)} %param.11, f32[5120]{0:T(1024)} %param.12, f32[4,2]{1,0:T(4,128)S(1)} %add_rsqrt_fusion.1), kind=kLoop, calls=%fused_computation.34 | loop fusion | flops 204800 | bytes 266272 | tf_op jit(solution)/shard_map/transpose | solution.py:480
  3.9 0.1 reshape.144
  4.0 0.7 copy.82
  4.8 51.3 %shard_map.109 = f32[8,10240]{1,0:T(8,128)} custom-call(f32[16,8,320]{2,1,0:T(8,128)} %bitcast.59, bf16[320,8192]{1,0:T(8,128)(2,1)} %wq_ref.1, bf16[320,1024]{1,0:T(8,128)(2,1)} %wk_ref.1, bf16[320,1024]{1,0:T(8,128)(2,1)} %wv_ref.1), custom_call_target="tpu_custom_call" | custom-call | tf_op jit(solution)/shard_map/pallas_call | solution.py:290
  56.1 1.0 %convert_element_type.37 = bf16[8,10240]{1,0:T(8,128)(2,1)S(1)} convert(f32[8,10240]{1,0:T(8,128)} %shard_map.109) | non-fusion elementwise | flops 81920 | bytes 491520 | tf_op jit(solution)/shard_map/convert_element_type | solution.py:492
  57.2 0.1 multiply_reduce_fusion.1
  57.3 0.1 copy.45
  57.7 0.1 multiply_reduce_fusion
  57.8 0.1 multiply_multiply_fusion
  58.0 0.1 fusion.11
  58.1 0.3 fusion.31
  58.4 0.9 %fusion.30 = (f32[2,8,32]{2,1,0:T(8,128)S(1)}, f32[2,8,32,512]{3,2,1,0:T(8,128)S(1)}) fusion(bf16[2,8,512,128]{3,2,1,0:T(8,128)(2,1)S(1)} %copy-done, pred[2,512]{1,0:T(4,128)(4,1)S(1)} %iota_compare_fusion, bf16[4,2,8,8,64]{4,3,2,1,0:T(8,128)(2,1)S(1)} %get-tuple-element.6, bf16[4,2,8,8,64]{4,3,2,1,0:T(8,128)(2,1)S(1)} %get-tuple-element.5), kind=kOutput, calls=%fused_computation.69 | convolution fusion | flops 68156928 | bytes 3279872 | tf_op jit(solution)/shard_map/rkqd,rkld->rkql/dot_general | solution.py:50
  59.4 0.3 fusion.4
  59.8 0.2 fusion.20
  60.0 0.5 fusion.2
  60.6 0.6 copy_bitcast_fusion.1.x_ref
  61.3 30.5 %shard_map.110 = f32[16,8,320]{2,1,0:T(8,128)} custom-call(bf16[4,16,1024]{2,1,0:T(8,128)(2,1)} %copy_bitcast_fusion.1.x_ref, bf16[320,8192]{1,0:T(8,128)(2,1)} %bitcast.56), custom_call_target="tpu_custom_call" | custom-call | tf_op jit(solution)/shard_map/pallas_call | solution.py:435
  91.8 1.0 %copy.50 = f32[8,16,320]{2,1,0:T(8,128)S(1)} copy(f32[8,16,320]{2,0,1:T(8,128)} %bitcast.60) | data formatting | bytes 327680 | tf_op jit(solution)/shard_map/transpose | solution.py:506
  92.8 0.2 reshape.139
  93.0 0.7 fusion.10
  (31 shorter events, 0.6 us)
Async XLA Ops:
  0.0 58.4 %copy-start = (bf16[2,8,512,128]{3,2,1,0:T(8,128)(2,1)S(1)}, bf16[2,8,512,128]{3,2,1,0:T(8,128)(2,1)}, u32[]{:S(2)}) copy-start(bf16[2,8,512,128]{3,2,1,0:T(8,128)(2,1)} %param.19) | copy-start | bytes 6291460
  4.8 52.6 %copy-start.2 = (f32[128]{0:T(128)S(1)}, f32[128]{0:T(128)}, u32[]{:S(2)}) copy-start(f32[128]{0:T(128)} %param.14) | copy-start | bytes 1540
  56.1 1.7 %copy-start.3 = (f32[128]{0:T(128)S(1)}, f32[128]{0:T(128)}, u32[]{:S(2)}) copy-start(f32[128]{0:T(128)} %param.13) | copy-start | bytes 1540
  58.4 1.6 %copy-start.4 = (bf16[2,8,512,128]{3,2,1,0:T(8,128)(2,1)S(1)}, bf16[2,8,512,128]{3,2,1,0:T(8,128)(2,1)}, u32[]{:S(2)}) copy-start(bf16[2,8,512,128]{3,2,1,0:T(8,128)(2,1)} %param.20) | copy-start | bytes 6291460
  61.3 31.7 %copy-start.1 = (bf16[4,2,5120]{2,1,0:T(2,128)(2,1)S(1)}, bf16[4,2,5120]{2,1,0:T(2,128)(2,1)}, u32[]{:S(2)}) copy-start(bf16[4,2,5120]{2,1,0:T(2,128)(2,1)} %param.11) | copy-start | bytes 245764

commit v4 on v3

--- a/solution.py
+++ b/solution.py
@@ -266,22 +266,22 @@
     side_copies = [None] * total
     short_copies = [None] * total
     long_copies = [None] * total
-    for tick in range(total + 6):
+    for tick in range(total + 8):
         if tick < total:
             side_copies[tick] = multiply(tick)
         if 0 <= tick - 1 < total:
             short_copies[tick - 1] = add_side(tick - 1, side_copies[tick - 1])
-        if 0 <= tick - 3 < total:
-            long_copies[tick - 3] = add_short(tick - 3, short_copies[tick - 3])
-        if 0 <= tick - 6 < total:
-            add_long(tick - 6, long_copies[tick - 6])
+        if 0 <= tick - 4 < total:
+            long_copies[tick - 4] = add_short(tick - 4, short_copies[tick - 4])
+        if 0 <= tick - 8 < total:
+            add_long(tick - 8, long_copies[tick - 8])
     for copy in scattered + sent:
         copy.wait_send()
 
 
 def project(blocks, w_query, w_key, w_value):
     own_rows, depth = blocks.shape[1:]
-    width = w_key.shape[1]
+    width = w_key.shape[1] // 2
     columns = w_query.shape[1] + w_key.shape[1] + w_value.shape[1]
     total = columns // width
     f32 = jnp.float32

time: 94 us -> 94.1 us (level)
  no operation moved by 1% of the time
where the time goes in v4:
time: 94.1 us; the launch traced here: 93.8 us
  Pallas kernels  82 us (87%)
  other arithmetic  6.67 us (7%)
  local copies, waits for them, and re-layouts  2.95 us (3%)
  matrix products  1.97 us (2%)
    pallas_call x1, Pallas kernels, project(): pl.pallas_call(functools.partial(project_kernel, width), out_shape=jax.Sh...  51.7 us
    pallas_call x1, Pallas kernels, output(): pl.pallas_call(output_kernel, out_shape=jax.ShapeDtypeStruct((OWNERS, blo...  30.3 us

profile of v4, /device:TPU:0, one launch (start us, length us, event | category | flops | bytes accessed | tf_op | source)
XLA Modules:
  0.0 93.8 jit_solution(14144982842696692232)
XLA Ops:
  0.0 0.8 convert_element_type.38
  0.9 0.7 iota_compare_fusion
  1.6 1.1 %fusion.7 = f32[4,2]{1,0:T(4,128)S(1)} fusion(bf16[4,2,5120]{2,1,0:T(2,128)(2,1)} %param.11), kind=kLoop, calls=%fused_computation.21 | loop fusion | flops 122872 | bytes 81952 | tf_op jit(solution)/shard_map/reduce_sum | solution.py:17
  2.7 0.1 multiply_cosine_fusion
  2.9 1.0 %fusion.17 = f32[4,2,5120]{2,1,0:T(2,128)S(1)} fusion(bf16[4,2,5120]{2,1,0:T(2,128)(2,1)} %param.11, f32[5120]{0:T(1024)} %param.12, f32[4,2]{1,0:T(4,128)S(1)} %add_rsqrt_fusion.1), kind=kLoop, calls=%fused_computation.34 | loop fusion | flops 204800 | bytes 266272 | tf_op jit(solution)/shard_map/transpose | solution.py:480
  3.9 0.1 reshape.144
  4.0 0.7 copy.82
  4.8 51.7 %shard_map.109 = f32[8,10240]{1,0:T(8,128)} custom-call(f32[16,8,320]{2,1,0:T(8,128)} %bitcast.59, bf16[320,8192]{1,0:T(8,128)(2,1)} %wq_ref.1, bf16[320,1024]{1,0:T(8,128)(2,1)} %wk_ref.1, bf16[320,1024]{1,0:T(8,128)(2,1)} %wv_ref.1), custom_call_target="tpu_custom_call" | custom-call | tf_op jit(solution)/shard_map/pallas_call | solution.py:290
  56.5 1.0 %convert_element_type.37 = bf16[8,10240]{1,0:T(8,128)(2,1)S(1)} convert(f32[8,10240]{1,0:T(8,128)} %shard_map.109) | non-fusion elementwise | flops 81920 | bytes 491520 | tf_op jit(solution)/shard_map/convert_element_type | solution.py:492
  57.6 0.1 copy.45
  57.7 0.1 fusion.18
  58.0 0.1 multiply_reduce_fusion
  58.2 0.1 multiply_multiply_fusion
  58.3 0.1 fusion.11
  58.5 0.3 fusion.31
  58.8 0.9 %fusion.30 = (f32[2,8,32]{2,1,0:T(8,128)S(1)}, f32[2,8,32,512]{3,2,1,0:T(8,128)S(1)}) fusion(bf16[2,8,512,128]{3,2,1,0:T(8,128)(2,1)S(1)} %copy-done, pred[2,512]{1,0:T(4,128)(4,1)S(1)} %iota_compare_fusion, bf16[4,2,8,8,64]{4,3,2,1,0:T(8,128)(2,1)S(1)} %get-tuple-element.6, bf16[4,2,8,8,64]{4,3,2,1,0:T(8,128)(2,1)S(1)} %get-tuple-element.5), kind=kOutput, calls=%fused_computation.69 | convolution fusion | flops 68156928 | bytes 3279872 | tf_op jit(solution)/shard_map/rkqd,rkld->rkql/dot_general | solution.py:50
  59.8 0.3 fusion.4
  60.1 0.2 fusion.20
  60.3 0.5 fusion.2
  61.0 0.6 copy_bitcast_fusion.1.x_ref
  61.6 30.3 %shard_map.110 = f32[16,8,320]{2,1,0:T(8,128)} custom-call(bf16[4,16,1024]{2,1,0:T(8,128)(2,1)} %copy_bitcast_fusion.1.x_ref, bf16[320,8192]{1,0:T(8,128)(2,1)} %bitcast.56), custom_call_target="tpu_custom_call" | custom-call | tf_op jit(solution)/shard_map/pallas_call | solution.py:435
  91.9 1.0 %copy.50 = f32[8,16,320]{2,1,0:T(8,128)S(1)} copy(f32[8,16,320]{2,0,1:T(8,128)} %bitcast.60) | data formatting | bytes 327680 | tf_op jit(solution)/shard_map/transpose | solution.py:506
  92.9 0.2 reshape.139
  93.1 0.7 fusion.10
  (31 shorter events, 0.6 us)
Async XLA Ops:
  0.0 58.7 %copy-start = (bf16[2,8,512,128]{3,2,1,0:T(8,128)(2,1)S(1)}, bf16[2,8,512,128]{3,2,1,0:T(8,128)(2,1)}, u32[]{:S(2)}) copy-start(bf16[2,8,512,128]{3,2,1,0:T(8,128)(2,1)} %param.19) | copy-start | bytes 6291460
  4.8 52.9 %copy-start.2 = (f32[128]{0:T(128)S(1)}, f32[128]{0:T(128)}, u32[]{:S(2)}) copy-start(f32[128]{0:T(128)} %param.14) | copy-start | bytes 1540
  56.5 1.7 %copy-start.3 = (f32[128]{0:T(128)S(1)}, f32[128]{0:T(128)}, u32[]{:S(2)}) copy-start(f32[128]{0:T(128)} %param.13) | copy-start | bytes 1540
  58.7 1.6 %copy-start.4 = (bf16[2,8,512,128]{3,2,1,0:T(8,128)(2,1)S(1)}, bf16[2,8,512,128]{3,2,1,0:T(8,128)(2,1)}, u32[]{:S(2)}) copy-start(bf16[2,8,512,128]{3,2,1,0:T(8,128)(2,1)} %param.20) | copy-start | bytes 6291460
  61.6 31.4 %copy-start.1 = (bf16[4,2,5120]{2,1,0:T(2,128)(2,1)S(1)}, bf16[4,2,5120]{2,1,0:T(2,128)(2,1)}, u32[]{:S(2)}) copy-start(bf16[4,2,5120]{2,1,0:T(2,128)(2,1)} %param.11) | copy-start | bytes 245764

commit v5 on v4

--- a/solution.py
+++ b/solution.py
@@ -123,7 +123,8 @@
 
 
 def by_side(where):
-    return (where[2] * SHORT + where[1]) * LONG + where[0]
+    pair = lax.rem(where[0], 2) * (LONG // 2) + where[0] // 2
+    return (where[2] * SHORT + where[1]) * LONG + pair
 
 
 def remote(src, dst, send_sem, recv_sem, where):
@@ -165,6 +166,8 @@
     second,
     from_short,
     third,
+    from_near,
+    fourth,
     from_long,
     load_sem,
     slab_send,
@@ -174,6 +177,7 @@
 ):
     me = place()
     long_index, short_index, side_index = me
+    upper, odd = long_index // 2, lax.rem(long_index, 2)
     loads = [
         pltpu.make_async_copy(src, dst, load_sem.at[i])
         for i, (src, dst) in enumerate(((wq_ref, wq), (wk_ref, wk), (wv_ref, wv)))
@@ -212,7 +216,7 @@
         product = jnp.dot(
             left, weight[:, start : start + width], preferred_element_type=jnp.float32
         )
-        first[c] = product.reshape(SIDE, SHORT, LONG, own_rows, width)
+        first[c] = product.reshape(SIDE, SHORT, 2, LONG // 2, own_rows, width)
         copy = remote(
             first.at[c, 1 - side_index],
             from_side.at[c],
@@ -241,30 +245,38 @@
     def add_short(c, arrived):
         arrived.wait_recv()
         third[c] = second[c, short_index] + from_short[c]
-        copies = []
-        for hop in range(1, LONG):
-            target = shifted(me, (hop, 0, 0))
-            copy = remote(
-                third.at[c, target[0]],
-                from_long.at[c, hop - 1],
-                send_sem.at[c, 1 + hop],
-                recv_sem.at[c, 1 + hop],
-                target,
-            )
-            copy.start()
-            copies.append(copy)
-        sent.extend(copies)
-        return copies
+        copy = remote(
+            third.at[c, 1 - odd],
+            from_near.at[c],
+            send_sem.at[c, 2],
+            recv_sem.at[c, 2],
+            (long_index + 1 - 2 * odd, short_index, side_index),
+        )
+        copy.start()
+        sent.append(copy)
+        return copy
+
+    def add_near(c, arrived):
+        arrived.wait_recv()
+        fourth[c] = third[c, odd] + from_near[c]
+        copy = remote(
+            fourth.at[c, 1 - upper],
+            from_long.at[c],
+            send_sem.at[c, 3],
+            recv_sem.at[c, 3],
+            shifted(me, (2, 0, 0)),
+        )
+        copy.start()
+        sent.append(copy)
+        return copy
 
     def add_long(c, arrived):
-        value = third[c, long_index]
-        for hop, copy in enumerate(arrived):
-            copy.wait_recv()
-            value = value + from_long[c, hop]
-        out_ref[:, c * width : (c + 1) * width] = value
+        arrived.wait_recv()
+        out_ref[:, c * width : (c + 1) * width] = fourth[c, upper] + from_long[c]
 
     side_copies = [None] * total
     short_copies = [None] * total
+    near_copies = [None] * total
     long_copies = [None] * total
     for tick in range(total + 8):
         if tick < total:
@@ -272,7 +284,9 @@
         if 0 <= tick - 1 < total:
             short_copies[tick - 1] = add_side(tick - 1, side_copies[tick - 1])
         if 0 <= tick - 4 < total:
-            long_copies[tick - 4] = add_short(tick - 4, short_copies[tick - 4])
+            near_copies[tick - 4] = add_short(tick - 4, short_copies[tick - 4])
+        if 0 <= tick - 6 < total:
+            long_copies[tick - 6] = add_near(tick - 6, near_copies[tick - 6])
         if 0 <= tick - 8 < total:
             add_long(tick - 8, long_copies[tick - 8])
     for copy in scattered + sent:
@@ -297,12 +311,14 @@
             pltpu.VMEM(w_key.shape, w_key.dtype),
             pltpu.VMEM(w_value.shape, w_value.dtype),
             pltpu.VMEM(blocks.shape, f32),
-            pltpu.VMEM((total, SIDE, SHORT, LONG, own_rows, width), f32),
-            pltpu.VMEM((total, SHORT, LONG, own_rows, width), f32),
-            pltpu.VMEM((total, SHORT, LONG, own_rows, width), f32),
-            pltpu.VMEM((total, LONG, own_rows, width), f32),
-            pltpu.VMEM((total, LONG, own_rows, width), f32),
-            pltpu.VMEM((total, LONG - 1, own_rows, width), f32),
+            pltpu.VMEM((total, SIDE, SHORT, 2, LONG // 2, own_rows, width), f32),
+            pltpu.VMEM((total, SHORT, 2, LONG // 2, own_rows, width), f32),
+            pltpu.VMEM((total, SHORT, 2, LONG // 2, own_rows, width), f32),
+            pltpu.VMEM((total, 2, LONG // 2, own_rows, width), f32),
+            pltpu.VMEM((total, 2, LONG // 2, own_rows, width), f32),
+            pltpu.VMEM((total, LONG // 2, own_rows, width), f32),
+            pltpu.VMEM((total, LONG // 2, own_rows, width), f32),
+            pltpu.VMEM((total, own_rows, width), f32),
             pltpu.SemaphoreType.DMA((3,)),
             pltpu.SemaphoreType.DMA((OWNERS,)),
             pltpu.SemaphoreType.DMA((OWNERS,)),

time: 94.1 us -> 96.7 us (1.028)
  Pallas kernels: 82 us -> 84.6 us
    pallas_call x1, Pallas kernels: 51.7 us -> 54.2 us  [project(): pl.pallas_call(functools.partial(project_kernel, width), out_shape=jax.Sh...]
where the time goes in v5:
time: 96.7 us; the launch traced here: 96.4 us
  Pallas kernels  84.6 us (87%)
  other arithmetic  6.67 us (7%)
  local copies, waits for them, and re-layouts  2.95 us (3%)
  matrix products  1.97 us (2%)
    pallas_call x1, Pallas kernels, project(): pl.pallas_call(functools.partial(project_kernel, width), out_shape=jax.Sh...  54.2 us
    pallas_call x1, Pallas kernels, output(): pl.pallas_call(output_kernel, out_shape=jax.ShapeDtypeStruct((OWNERS, blo...  30.4 us

profile of v5, /device:TPU:0, one launch (start us, length us, event | category | flops | bytes accessed | tf_op | source)
XLA Modules:
  0.0 96.4 jit_solution(3972305683474372936)
XLA Ops:
  0.0 0.8 convert_element_type.38
  0.9 0.7 iota_compare_fusion
  1.6 1.1 %fusion.7 = f32[4,2]{1,0:T(4,128)S(1)} fusion(bf16[4,2,5120]{2,1,0:T(2,128)(2,1)} %param.11), kind=kLoop, calls=%fused_computation.21 | loop fusion | flops 122872 | bytes 81952 | tf_op jit(solution)/shard_map/reduce_sum | solution.py:17
  2.7 0.1 multiply_cosine_fusion
  2.9 1.0 %fusion.17 = f32[4,2,5120]{2,1,0:T(2,128)S(1)} fusion(bf16[4,2,5120]{2,1,0:T(2,128)(2,1)} %param.11, f32[5120]{0:T(1024)} %param.12, f32[4,2]{1,0:T(4,128)S(1)} %add_rsqrt_fusion.1), kind=kLoop, calls=%fused_computation.34 | loop fusion | flops 204800 | bytes 266272 | tf_op jit(solution)/shard_map/transpose | solution.py:496
  3.9 0.1 reshape.144
  4.0 0.7 copy.82
  4.8 54.2 %shard_map.109 = f32[8,10240]{1,0:T(8,128)} custom-call(f32[16,8,320]{2,1,0:T(8,128)} %bitcast.59, bf16[320,8192]{1,0:T(8,128)(2,1)} %wq_ref.1, bf16[320,1024]{1,0:T(8,128)(2,1)} %wk_ref.1, bf16[320,1024]{1,0:T(8,128)(2,1)} %wv_ref.1), custom_call_target="tpu_custom_call" | custom-call | tf_op jit(solution)/shard_map/pallas_call | solution.py:304
  59.0 1.0 %convert_element_type.37 = bf16[8,10240]{1,0:T(8,128)(2,1)S(1)} convert(f32[8,10240]{1,0:T(8,128)} %shard_map.109) | non-fusion elementwise | flops 81920 | bytes 491520 | tf_op jit(solution)/shard_map/convert_element_type | solution.py:508
  60.0 0.1 multiply_reduce_fusion.1
  60.1 0.1 copy.45
  60.5 0.1 multiply_reduce_fusion
  60.7 0.1 multiply_multiply_fusion
  60.8 0.1 fusion.11
  61.0 0.3 fusion.31
  61.3 0.9 fusion.30
  62.3 0.3 fusion.4
  62.6 0.2 fusion.20
  62.9 0.5 fusion.2
  63.5 0.6 copy_bitcast_fusion.1.x_ref
  64.2 30.4 %shard_map.110 = f32[16,8,320]{2,1,0:T(8,128)} custom-call(bf16[4,16,1024]{2,1,0:T(8,128)(2,1)} %copy_bitcast_fusion.1.x_ref, bf16[320,8192]{1,0:T(8,128)(2,1)} %bitcast.56), custom_call_target="tpu_custom_call" | custom-call | tf_op jit(solution)/shard_map/pallas_call | solution.py:451
  94.5 1.0 %copy.50 = f32[8,16,320]{2,1,0:T(8,128)S(1)} copy(f32[8,16,320]{2,0,1:T(8,128)} %bitcast.60) | data formatting | bytes 327680 | tf_op jit(solution)/shard_map/transpose | solution.py:522
  95.5 0.2 reshape.139
  95.7 0.7 fusion.10
  (31 shorter events, 0.6 us)
Async XLA Ops:
  0.0 61.3 %copy-start = (bf16[2,8,512,128]{3,2,1,0:T(8,128)(2,1)S(1)}, bf16[2,8,512,128]{3,2,1,0:T(8,128)(2,1)}, u32[]{:S(2)}) copy-start(bf16[2,8,512,128]{3,2,1,0:T(8,128)(2,1)} %param.19) | copy-start | bytes 6291460
  4.8 55.5 %copy-start.2 = (f32[128]{0:T(128)S(1)}, f32[128]{0:T(128)}, u32[]{:S(2)}) copy-start(f32[128]{0:T(128)} %param.14) | copy-start | bytes 1540
  59.0 1.7 %copy-start.3 = (f32[128]{0:T(128)S(1)}, f32[128]{0:T(128)}, u32[]{:S(2)}) copy-start(f32[128]{0:T(128)} %param.13) | copy-start | bytes 1540
  61.3 1.6 %copy-start.4 = (bf16[2,8,512,128]{3,2,1,0:T(8,128)(2,1)S(1)}, bf16[2,8,512,128]{3,2,1,0:T(8,128)(2,1)}, u32[]{:S(2)}) copy-start(bf16[2,8,512,128]{3,2,1,0:T(8,128)(2,1)} %param.20) | copy-start | bytes 6291460
  64.2 31.5 %copy-start.1 = (bf16[4,2,5120]{2,1,0:T(2,128)(2,1)S(1)}, bf16[4,2,5120]{2,1,0:T(2,128)(2,1)}, u32[]{:S(2)}) copy-start(bf16[4,2,5120]{2,1,0:T(2,128)(2,1)} %param.11) | copy-start | bytes 245764
